TPU v7x, 32 devices: a whole 2x2x4 slice. The times are simulated.
32 devices in a mesh: pairs: 8 (over z, x), sect: 4 (over y, core).
Axes of the slice: x: 2, y: 2, z: 4, core: 2. Of those that a mesh axis runs over, the one named last changes fastest.
Arguments:
- wavefunction: bfloat16 [4096, 1024], P('sect'), may hold values from -6 to 6
- left_normal: bfloat16 [16, 8, 512, 512], P('pairs', 'sect'), may hold values from -0.0625 to 0.0625
- left_comp: bfloat16 [16, 8, 512, 512], P('pairs', 'sect'), may hold values from -0.0625 to 0.0625
- right_comp: bfloat16 [16, 2, 512, 512], P('pairs'), may hold values from -0.25 to 0.25
- right_normal: bfloat16 [16, 2, 512, 512], P('pairs'), may hold values from -0.25 to 0.25
- pair_shift: int32 [16], P('pairs'), may hold values from 0 to 1
- pair_count: int32 [8], P('pairs'), may hold values from 1 to 2, as said below
- sector_rows: int32 [8], P('sect'), may hold values from 128 to 512, as said below
Outputs:
- sigma: bfloat16 [4096, 1024], P(('sect', 'pairs'))
Inputs may be any that keep to these rules, and one draw needn't show every extreme that they name: Index i of pairs holds pair slots i * 2 to (i + 1) * 2 - 1, of which the first pair_count[i] are live; some index has all 2 live. Rows of sector s at or beyond sector_rows[s] are padding; some sector uses all 512 rows.
All inputs are finite; a program needn't handle non-finite values.
Results may differ from a plain program's by a relative error of at most 0.005.
Values may be sent and summed in bfloat16 or wider, within the bound.
A program may use at most 128 MiB of HBM per device.

v0:
```python
import jax
import jax.numpy as jnp
from jax import lax
from jax.sharding import PartitionSpec as P


def shifted(value, axis, steps):
    count = lax.axis_size(axis)
    leading, last = (max(0, -steps), min(count, count - steps))
    return lax.ppermute(value, axis, [(source, source + steps) for source in range(leading, last)])


def local(
    wavefunction,
    left_normal,
    left_comp,
    right_comp,
    right_normal,
    pair_shift,
    pair_count,
    sector_rows,
):
    sec_dev = left_normal.shape[1]
    width = left_normal.shape[3]
    blocks = right_comp.shape[1]
    block_width = right_comp.shape[3]
    columns = blocks * block_width
    row_keep = jnp.arange(width, dtype=jnp.int32)[None, :] < sector_rows[:, None]
    blocked = wavefunction.reshape(sec_dev, width, columns)
    masked = jnp.where(row_keep[:, :, None], blocked, jnp.zeros((), jnp.bfloat16))
    lower_block = shifted(masked[sec_dev - 1], "sect", 1)
    earlier = jnp.concatenate([lower_block[None], masked[: sec_dev - 1]], axis=0)

    def right_apply(left_part, offset, right_ops):
        rolled = jnp.roll(left_part.reshape(sec_dev, width, blocks, block_width), -offset, axis=2)
        product = jnp.einsum(
            "sikb,kcb->sikc", rolled, right_ops, preferred_element_type=jnp.float32
        )
        return product.reshape(sec_dev * width, columns)

    def add_pair(slot_index, totals):
        normal_left = jnp.einsum(
            "sij,sjk->sik", left_normal[slot_index], masked, preferred_element_type=jnp.float32
        ).astype(jnp.bfloat16)
        comp_left = jnp.einsum(
            "sij,sjk->sik", left_comp[slot_index], earlier, preferred_element_type=jnp.float32
        ).astype(jnp.bfloat16)
        offset = pair_shift[slot_index]
        normal_next = totals[0] + right_apply(normal_left, offset, right_comp[slot_index])
        comp_next = totals[1] + right_apply(comp_left, offset, right_normal[slot_index])
        return (normal_next, comp_next)

    empty = jnp.zeros((sec_dev * width, columns), jnp.float32)
    normal_sum, comp_sum = lax.fori_loop(0, pair_count[0], add_pair, (empty, empty))
    normal_part = lax.psum_scatter(normal_sum, "pairs", scatter_dimension=0, tiled=True)
    comp_part = lax.psum_scatter(comp_sum, "pairs", scatter_dimension=0, tiled=True)
    combined = normal_part + comp_part
    own_rows = combined.shape[0]
    row_start = lax.axis_index("pairs") * own_rows
    keep_flat = row_keep.reshape(sec_dev * width)
    keep_mine = lax.dynamic_slice_in_dim(keep_flat, row_start, own_rows, 0)
    combined = jnp.where(keep_mine[:, None], combined, jnp.zeros((), jnp.float32))
    return combined.astype(jnp.bfloat16)


def solution(mesh):
    placed = (
        P("sect", None),
        P("pairs", "sect", None, None),
        P("pairs", "sect", None, None),
        P("pairs", None, None, None),
        P("pairs", None, None, None),
        P("pairs"),
        P("pairs"),
        P("sect"),
    )
    return jax.shard_map(
        local, mesh=mesh, in_specs=placed, out_specs=P(("sect", "pairs"), None), check_vma=False
    )
```

profile of v0, /device:TPU:4, one launch (start us, length us, event | category | flops | bytes accessed | tf_op | source)
XLA Modules:
  0.0 226.7 jit_solution(11097110254809830858)
XLA Ops:
  6.5 0.0 reduce-scatter.2.cloned.1.call-start
  6.5 0.7 iota_compare_fusion
  7.3 1.8 broadcast_select_fusion
  9.1 1.2 slice_bitcast_fusion
  10.3 1.9 collective-permute-start
  12.2 14.5 %collective-permute-done = bf16[512,1024]{1,0:T(8,128)(2,1)} collective-permute-done((bf16[512,1024]{1,0:T(8,128)(2,1)}, bf16[512,1024]{1,0:T(8,128)(2,1)}, u32[]{:S(2)}, u32[]{:S(2)}) %collective-permute-start) | collective-permute-done | bytes 1048608 | tf_op jit(solution)/shard_map/ppermute | solution.py:10
  26.7 2.7 %pad_maximum_fusion = bf16[2,512,1024]{2,1,0:T(8,128)(2,1)} fusion(bf16[1,512,1024]{2,1,0:T(8,128)(2,1)S(1)} %get-tuple-element.90, bf16[1,512,1024]{2,1,0:T(8,128)(2,1)} %bitcast.14), kind=kLoop, calls=%fused_computation.26 | loop fusion | flops 1048576 | bytes 4194304 | tf_op jit(solution)/shard_map/concatenate | solution.py:32
  29.4 2.5 %broadcast_in_dim.35.clone = f32[1024,1024]{1,0:T(8,128)} broadcast(f32[]{:T(128)} %constant.38.clone.1), dimensions={} | broadcast | bytes 4194308 | tf_op jit(solution)/shard_map/broadcast_in_dim | solution.py:53
  31.9 0.0 copy-start.7
  31.9 2.5 %broadcast_in_dim.35 = f32[1024,1024]{1,0:T(8,128)} broadcast(f32[]{:T(128)} %constant.38.clone.1), dimensions={} | broadcast | bytes 4194308 | tf_op jit(solution)/shard_map/broadcast_in_dim | solution.py:53
  34.4 0.0 copy-done.7
  34.4 44.0 %while.12 = (s32[]{:T(128)}, f32[1024,1024]{1,0:T(8,128)}, f32[1024,1024]{1,0:T(8,128)}, s32[]{:T(128)}, bf16[2,2,512,512]{3,2,1,0:T(8,128)(2,1)}, /*index=5*/bf...) while((s32[]{:T(128)}, f32[1024,1024]{1,0:T(8,128)}, ...), condition=%wide.region_1.3_spmd, body=%wide.region_0.2_spmd.sunk | while | flops 4307550208 | bytes 184549968 | solution.py:54
  35.1 0.6 dynamic_slice.78
  36.3 3.2 %convolution_convert_fusion.5 = bf16[2,512,1024]{2,1,0:T(8,128)(2,1)S(1)} fusion(bf16[2,512,1024]{2,1,0:T(8,128)(2,1)} %get-tuple-element.199, bf16[2,2,512,512]{3,2,1,0:T(8,128)(2,1)} %get-tuple-element.198, s32[]{:T(128)S(6)} %select_n.42), kind=kOutput, calls=%fused_computation.10.clone.1 | convolution fusion | flops 1074790400 | bytes 5242884 | tf_op jit(solution)/shard_map/while/body/sij,sjk->sik/dot_general | solution.py:45
  39.4 0.0 copy-start.6
  39.5 0.2 copy.38
  39.6 1.4 copy-done.6
  41.0 3.3 %convolution_bitcast_fusion.5 = f32[2,512,2,512]{1,3,0,2:T(8,128)} fusion(s32[]{:T(128)S(6)} %select_n.44, bf16[2,512,2,512]{3,1,0,2:T(8,128)(2,1)S(1)} %bitcast.83, bf16[2,2,512,512]{3,2,1,0:T(8,128)(2,1)S(1)} %copy-done.6, s32[]{:T(128)S(6)} %select_n.42), kind=kOutput, calls=%fused_computation.4.clone.1 | convolution fusion | flops 1077936128 | bytes 7340040 | tf_op jit(solution)/shard_map/while/body/sikb,kcb->sikc/dot_general | solution.py:36
  44.4 7.3 %copy.39 = f32[2,512,2,512]{3,2,1,0:T(2,128)} copy(f32[2,512,2,512]{1,3,0,2:T(8,128)} %convolution_bitcast_fusion.5) | data formatting | bytes 8388608 | tf_op jit(solution)/shard_map/while/body/sikb,kcb->sikc/transpose | solution.py:36
  51.7 0.0 copy-start
  51.7 3.4 %copy.40 = f32[128,8,2,512]{3,1,2,0:T(8,128)S(1)} copy(f32[128,8,2,512]{3,2,1,0:T(2,128)} %bitcast.80) | data formatting | bytes 8388608 | tf_op jit(solution)/shard_map/while
  55.0 0.1 copy-done
  55.1 0.0 copy-start.5
  55.1 1.5 add.54
  56.6 0.1 copy-done.5
  56.7 0.0 copy-start.1
  56.7 1.3 convolution_convert_fusion.4
  58.0 0.7 copy-done.1
  58.7 0.0 copy-start.4
  58.7 0.2 copy.35
  58.8 1.4 copy-done.4
  60.3 3.3 %convolution_bitcast_fusion.4 = f32[2,512,2,512]{1,3,0,2:T(8,128)} fusion(s32[]{:T(128)S(6)} %select_n.44, bf16[2,512,2,512]{3,1,0,2:T(8,128)(2,1)S(1)} %bitcast.82, bf16[2,2,512,512]{3,2,1,0:T(8,128)(2,1)S(1)} %copy-done.4, s32[]{:T(128)S(6)} %select_n.42), kind=kOutput, calls=%fused_computation.5.clone.1 | convolution fusion | flops 1077936128 | bytes 7340040 | tf_op jit(solution)/shard_map/while/body/sikb,kcb->sikc/dot_general | solution.py:36
  63.6 7.3 %copy.36 = f32[2,512,2,512]{3,2,1,0:T(2,128)} copy(f32[2,512,2,512]{1,3,0,2:T(8,128)} %convolution_bitcast_fusion.4) | data formatting | bytes 8388608 | tf_op jit(solution)/shard_map/while/body/sikb,kcb->sikc/transpose | solution.py:36
  70.9 0.0 copy-start.2
  70.9 3.4 %copy.37 = f32[128,8,2,512]{3,1,2,0:T(8,128)S(1)} copy(f32[128,8,2,512]{3,2,1,0:T(2,128)} %bitcast.81) | data formatting | bytes 8388608 | tf_op jit(solution)/shard_map/while
  74.2 0.1 copy-done.2
  74.3 1.5 add.53
  75.8 0.0 copy-start.3
  75.8 1.9 copy-done.3
  78.4 6.8 %add.38 = f32[1024,1024]{1,0:T(8,128)} add(f32[1024,1024]{1,0:T(8,128)} %get-tuple-element.65, f32[1024,1024]{1,0:T(8,128)} %get-tuple-element.66) | non-fusion elementwise | flops 1048576 | bytes 12582912 | tf_op jit(solution)/shard_map/add | solution.py:57
  85.2 0.0 reduce-scatter.2.cloned.1.call-update
  85.3 0.1 dynamic_slice.21
  85.4 132.7 %reduce-scatter.2.cloned.1.call-done = f32[128,1024]{1,0:T(8,128)} async-done(((f32[1024,1024]{1,0:T(8,128)}), f32[128,1024]{1,0:T(8,128)}) %reduce-scatter.2.cloned.1.call-update) | async-done | bytes 524304 | tf_op jit(solution)/shard_map/reduce_scatter | solution.py:55
  218.0 1.8 select_convert_fusion
  (1 shorter events, 0.0 us)
Async XLA Ops:
  6.5 211.5 %reduce-scatter.2.cloned.1.call-start = ((), (), s32[]{:S(2)}) async-start(), calls=%async_computation.1 | async-start | bytes 4718592 | tf_op jit(solution)/shard_map/reduce_scatter | solution.py:55
  10.3 16.4 %collective-permute-start = (bf16[512,1024]{1,0:T(8,128)(2,1)}, bf16[512,1024]{1,0:T(8,128)(2,1)}, u32[]{:S(2)}, u32[]{:S(2)}) collective-permute-start(bf16[512,1024]{1,0:T(8,128)(2,1)} %get-tuple-element.89), channel_id=1, source_target_pairs={{0,1},{1,2},{2,3},{4,5},{5,6},{6,7},{8,9},{9,10},{10,11},{12,13},{... | collective-permute-start | bytes 3145736 | tf_op jit(solution)/shard_map/ppermute | solution.py:10
  31.9 2.5 %copy-start.7 = (s32[2]{0:T(128)S(1)}, s32[2]{0:T(128)}, u32[]{:S(2)}) copy-start(s32[2]{0:T(128)} %param.17) | copy-start | bytes 28
  39.4 1.6 copy-start.6
  51.7 3.4 %copy-start = (f32[1024,1024]{1,0:T(8,128)S(1)}, f32[1024,1024]{1,0:T(8,128)}, u32[]{:S(2)}) copy-start(f32[1024,1024]{1,0:T(8,128)} %get-tuple-element.176) | copy-start | bytes 12582916 | tf_op jit(solution)/shard_map/while
  55.1 1.6 copy-start.5
  56.7 2.0 copy-start.1
  58.7 1.6 copy-start.4
  70.9 3.4 %copy-start.2 = (f32[1024,1024]{1,0:T(8,128)S(1)}, f32[1024,1024]{1,0:T(8,128)}, u32[]{:S(2)}) copy-start(f32[1024,1024]{1,0:T(8,128)} %get-tuple-element.175) | copy-start | bytes 12582916 | tf_op jit(solution)/shard_map/while
  75.8 2.0 copy-start.3
Sparse Core Ops, SparseCore 0:
  85.4 132.6 reduce-scatter.1
where the time goes:
time: 229 us; the launch traced here: 227 us
  waiting for transfers between devices  147 us (64%)
  local copies, waits for them, and re-layouts  34.2 us (15%)
  other arithmetic  16.9 us (7%)
  between operations  13.4 us (6%)
  matrix products  11.1 us (5%)
    reduce_scatter x1, waiting for transfers between devices, local(): lax.psum_scatter(normal_sum, 'pairs', scatter_dimension=0, tiled=True)  133 us
    transpose x2, local copies, waits for them, and re-layouts, right_apply(): jnp.einsum('sikb,kcb->sikc', rolled, right_ops, preferred_element_type=jn...  14.6 us
    ppermute x1, waiting for transfers between devices, shifted(): lax.ppermute(value, axis, [(source, source + steps) for source in range(l...  14.5 us
    while x16, local copies, waits for them, and re-layouts  12.5 us
    add x1, other arithmetic, local(): combined = normal_part + comp_part  6.8 us
    dot_general x2, matrix products, right_apply(): jnp.einsum('sikb,kcb->sikc', rolled, right_ops, preferred_element_type=jn...  6.62 us
    broadcast_in_dim x2, local copies, waits for them, and re-layouts, local(): empty = jnp.zeros((sec_dev * width, columns), jnp.float32)  4.97 us
  transfers between devices with their start and end apart: 2, of which 2 were waited for; matrix products, arithmetic and copies ran while one was open for 0% of the time, Pallas kernels for 0%

commit v1 on v0

v1 whole, which is shorter than its diff:
```python
import functools

import jax
import jax.numpy as jnp
from jax import lax
from jax.experimental import pallas as pl
from jax.experimental.pallas import tpu as pltpu
from jax.sharding import PartitionSpec as P

MESH = pl.DeviceIdType.MESH
F32 = jnp.float32
BF16 = jnp.bfloat16
NT = (((1,), (1,)), ((), ()))


def x_size(count):
    return 1 << ((count.bit_length() - 1) // 2)


def kernel(
    nz,
    nx,
    ns,
    shift_ref,
    count_ref,
    rows_ref,
    wave,
    left_normal,
    left_comp,
    right_comp,
    right_normal,
    out_ref,
    waves,
    lefts,
    rights,
    applied,
    total,
    own,
    x_out,
    x_in,
    z_out,
    z_in,
    far_in,
    load_sem,
    halo_send,
    halo_recv,
    x_send,
    x_recv,
    z_send,
    z_recv,
    far_recv,
):
    pair_dev, sec_dev, width, _ = left_normal.shape
    blocks, cols = right_comp.shape[1], right_comp.shape[2]
    chunk = sec_dev * width // nz
    part = chunk // nx
    me = lax.axis_index("pairs")
    sect = lax.axis_index("sect")
    z = me // nx
    x = lax.rem(me, nx)
    partner = z + 1 - 2 * lax.rem(z, 2)

    loads = {}

    def load(name, source, target):
        copy = pltpu.make_async_copy(source, target, load_sem.at[len(loads)])
        copy.start()
        loads[name] = copy

    for s in reversed(range(sec_dev)):
        load(("wave", s), wave.at[pl.ds(s * width, width)], waves.at[s + 1])
    for s in reversed(range(sec_dev)):
        for p in range(pair_dev):
            load(("normal", s, p), left_normal.at[p, s], lefts.at[0, p, s])
            load(("comp", s, p), left_comp.at[p, s], lefts.at[1, p, s])
        if s == sec_dev - 1:
            load("right_comp", right_comp, rights.at[0])
            load("right_normal", right_normal, rights.at[1])

    barrier = pltpu.get_barrier_semaphore()
    for d in range(1, nx):
        pl.semaphore_signal(barrier, inc=1, device_id=(z * nx + lax.rem(x + d, nx), sect), device_id_type=MESH)
    for d in range(1, nz):
        pl.semaphore_signal(barrier, inc=1, device_id=(lax.rem(z + d, nz) * nx + x, sect), device_id_type=MESH)
    for d in (1, ns - 1):
        pl.semaphore_signal(barrier, inc=1, device_id=(me, lax.rem(sect + d, ns)), device_id_type=MESH)

    def mask(s):
        loads[("wave", s)].wait()
        step = 64

        def body(i, _):
            at = pl.ds(i * step, step)
            keep = lax.broadcasted_iota(jnp.int32, (step, blocks * cols), 0) + i * step < rows_ref[s]
            value = waves[s + 1, at, :].astype(F32)
            waves[s + 1, at, :] = jnp.where(keep, value, 0.0).astype(BF16)
            return 0

        lax.fori_loop(0, width // step, body, 0)

    mask(sec_dev - 1)
    pl.semaphore_wait(barrier, nx - 1 + nz - 1 + 2)
    halo = pltpu.make_async_remote_copy(
        src_ref=waves.at[sec_dev],
        dst_ref=waves.at[0],
        send_sem=halo_send,
        recv_sem=halo_recv,
        device_id=(me, lax.rem(sect + 1, ns)),
        device_id_type=MESH,
    )

    @pl.when(sect < ns - 1)
    def _():
        halo.start()

    @pl.when(sect == 0)
    def _():
        waves[0] = jnp.zeros((width, blocks * cols), BF16)

    for s in reversed(range(sec_dev - 1)):
        mask(s)

    def order(k):
        down = nz - 1 - k
        return jnp.where(k == nz - 1, z, jnp.where(down > z, down, down - 1))

    def x_copy(c, d, j):
        return pltpu.make_async_remote_copy(
            src_ref=x_out.at[c, d - 1, j],
            dst_ref=x_in.at[c, d - 1, j],
            send_sem=x_send.at[c, d - 1, j],
            recv_sem=x_recv.at[c, d - 1, j],
            device_id=(z * nx + lax.rem(x + d, nx), sect),
            device_id_type=MESH,
        )

    def z_copy(c, j):
        return pltpu.make_async_remote_copy(
            src_ref=z_out.at[c, j],
            dst_ref=z_in.at[c, j],
            send_sem=z_send.at[c, j],
            recv_sem=z_recv.at[c, j],
            device_id=(partner * nx + x, sect),
            device_id_type=MESH,
        )

    def far_copy(c, j, slot):
        return pltpu.make_async_remote_copy(
            src_ref=z_out.at[c, j],
            dst_ref=far_in.at[slot, j],
            send_sem=z_send.at[c, j],
            recv_sem=far_recv.at[slot, j],
            device_id=(c * nx + x, sect),
            device_id_type=MESH,
        )

    def combines(c):
        above = (c // 2 > z // 2) & (lax.rem(z, 2) == 1)
        below = (c // 2 < z // 2) & (lax.rem(z, 2) == 0)
        return above | below

    def compute(k):
        c = order(k)
        s = c * chunk // width
        at = pl.ds(pl.multiple_of(c * chunk - s * width, chunk), chunk)
        for p in range(pair_dev):
            live = p < count_ref[0]
            offset = shift_ref[p]
            for kind in range(2):
                ops = lefts[kind, p, s, at, :]
                value = jnp.dot(ops, waves[s + 1 - kind], preferred_element_type=F32)
                value = jnp.where(live, value, 0.0).astype(BF16)
                pieces = [value[:, j * cols : (j + 1) * cols] for j in range(blocks)]
                for j in range(blocks):
                    piece = pieces[j]
                    for o in range(1, blocks):
                        piece = jnp.where(offset == o, pieces[(j + o) % blocks], piece)
                    applied[j, kind, p] = piece
        for j in range(blocks):
            result = None
            for kind in range(2):
                for p in range(pair_dev):
                    term = lax.dot_general(applied[j, kind, p], rights[kind, p, j], NT, preferred_element_type=F32)
                    result = term if result is None else result + term
            total[...] = result
            own[c, j] = total[pl.ds(pl.multiple_of(x * part, part), part), :]
            for d in range(1, nx):
                to = lax.rem(x + d, nx)
                x_out[c, d - 1, j] = total[pl.ds(pl.multiple_of(to * part, part), part), :].astype(BF16)
                x_copy(c, d, j).start()

    def x_sum(k):
        c = order(k)
        for j in range(blocks):
            value = own[c, j]
            for d in range(1, nx):
                x_copy(c, d, j).wait_recv()
                value = value + x_in[c, d - 1, j].astype(F32)
            own[c, j] = value

            @pl.when((c != z) & jnp.logical_not(combines(c)))
            def _():
                z_out[c, j] = value.astype(BF16)
                z_copy(c, j).start()

    def z_sum(k):
        c = order(k)

        @pl.when((c != z) & combines(c))
        def _():
            for j in range(blocks):
                z_copy(c, j).wait_recv()
                z_out[c, j] = (own[c, j] + z_in[c, j].astype(F32)).astype(BF16)
                far_copy(c, j, z // 2).start()

    last = sec_dev - 1
    for p in range(pair_dev):
        loads[("normal", last, p)].wait()
        loads[("comp", last, p)].wait()
    loads["right_comp"].wait()
    loads["right_normal"].wait()
    for s in range(last):
        for p in range(pair_dev):
            loads[("normal", s, p)].wait()
            loads[("comp", s, p)].wait()

    halo_step = nz - nz // sec_dev - jnp.where(z >= nz // sec_dev, 1, 0)

    def step(k, _):
        @pl.when((k == halo_step) & (sect > 0))
        def _():
            halo.wait_recv()

        @pl.when(k < nz)
        def _():
            compute(k)

        @pl.when((k >= 1) & (k <= nz))
        def _():
            x_sum(k - 1)

        @pl.when(k >= 2)
        def _():
            z_sum(k - 2)

        return 0

    lax.fori_loop(0, nz + 1, step, 0)

    for j in range(blocks):
        value = own[z, j]
        z_copy(z, j).wait_recv()
        value = value + z_in[z, j].astype(F32)
        for d in range(1, nz // 2):
            slot = lax.rem(z // 2 + d, nz // 2)
            far_copy(z, j, slot).wait_recv()
            value = value + far_in[slot, j].astype(F32)
        out_ref[:, j * cols : (j + 1) * cols] = value.astype(BF16)

    @pl.when(sect < ns - 1)
    def _():
        halo.wait_send()

    def drain(k, _):
        c = order(k)
        for j in range(blocks):
            for d in range(1, nx):
                x_copy(c, d, j).wait_send()

            @pl.when(c != z)
            def _():
                z_copy(c, j).wait_send()

        return 0

    lax.fori_loop(0, nz, drain, 0)


def solution(mesh):
    n_pairs, ns = mesh.shape["pairs"], mesh.shape["sect"]
    nx = x_size(n_pairs)
    nz = n_pairs // nx

    def local(wavefunction, left_normal, left_comp, right_comp, right_normal, pair_shift, pair_count, sector_rows):
        pair_dev, sec_dev, width, _ = left_normal.shape
        blocks, cols = right_comp.shape[1], right_comp.shape[2]
        chunk = sec_dev * width // nz
        part = chunk // nx
        dma = pltpu.SemaphoreType.DMA
        smem = pl.BlockSpec(memory_space=pltpu.SMEM)
        hbm = pl.BlockSpec(memory_space=pl.ANY)
        summed = pl.pallas_call(
            functools.partial(kernel, nz, nx, ns),
            out_shape=jax.ShapeDtypeStruct((part, blocks * cols), BF16),
            in_specs=[smem] * 3 + [hbm] * 5,
            out_specs=pl.BlockSpec(memory_space=pltpu.VMEM),
            scratch_shapes=[
                pltpu.VMEM((sec_dev + 1, width, blocks * cols), BF16),
                pltpu.VMEM((2, pair_dev, sec_dev, width, width), BF16),
                pltpu.VMEM((2, pair_dev, blocks, cols, cols), BF16),
                pltpu.VMEM((blocks, 2, pair_dev, chunk, cols), BF16),
                pltpu.VMEM((chunk, cols), F32),
                pltpu.VMEM((nz, blocks, part, cols), F32),
                pltpu.VMEM((nz, nx - 1, blocks, part, cols), BF16),
                pltpu.VMEM((nz, nx - 1, blocks, part, cols), BF16),
                pltpu.VMEM((nz, blocks, part, cols), BF16),
                pltpu.VMEM((nz, blocks, part, cols), BF16),
                pltpu.VMEM((nz // 2, blocks, part, cols), BF16),
                dma((sec_dev + 2 * sec_dev * pair_dev + 2,)),
                dma,
                dma,
                dma((nz, nx - 1, blocks)),
                dma((nz, nx - 1, blocks)),
                dma((nz, blocks)),
                dma((nz, blocks)),
                dma((nz // 2, blocks)),
            ],
            compiler_params=pltpu.CompilerParams(
                collective_id=0, has_side_effects=True, vmem_limit_bytes=48 * 2**20
            ),
        )(pair_shift, pair_count, sector_rows, wavefunction, left_normal, left_comp, right_comp, right_normal)
        first = lax.axis_index("pairs") * part
        kept = sector_rows[first // width]
        row = lax.broadcasted_iota(jnp.int32, (part, blocks * cols), 0) + lax.rem(first, width)
        return jnp.where(row < kept, summed, jnp.zeros((), BF16))

    placed = (
        P("sect", None),
        P("pairs", "sect", None, None),
        P("pairs", "sect", None, None),
        P("pairs", None, None, None),
        P("pairs", None, None, None),
        P("pairs"),
        P("pairs"),
        P("sect"),
    )
    return jax.shard_map(
        local, mesh=mesh, in_specs=placed, out_specs=P(("sect", "pairs"), None), check_vma=False
    )
```

time: 229 us -> 48.5 us (0.21)
  waiting for transfers between devices: 147 us -> 0 us
  Pallas kernels: 0 us -> 39.9 us
  local copies, waits for them, and re-layouts: 34.2 us -> 5.73 us
  other arithmetic: 16.9 us -> 1.44 us
  between operations: 13.4 us -> 0.68 us
  matrix products: 11.1 us -> 0 us
    reduce_scatter x1 -> x0, waiting for transfers between devices: 133 us -> none  [local(): lax.psum_scatter(normal_sum, 'pairs', scatter_dimension=0, tiled=True)]
    pallas_call x0 -> x1, Pallas kernels: none -> 39.9 us  [local(): pl.pallas_call(functools.partial(kernel, nz, nx, ns), out_shape=jax.Shape...]
    transpose x2 -> x0, local copies, waits for them, and re-layouts: 14.6 us -> none  [right_apply(): jnp.einsum('sikb,kcb->sikc', rolled, right_ops, preferred_element_type=jn...]
    ppermute x1 -> x0, waiting for transfers between devices: 14.5 us -> none  [shifted(): lax.ppermute(value, axis, [(source, source + steps) for source in range(l...]
    while x16 -> x0, local copies, waits for them, and re-layouts: 12.5 us -> none
    dot_general x4 -> x0, matrix products: 11.1 us -> none  [the longest x2 6.62 us: right_apply(): jnp.einsum('sikb,kcb->sikc', rolled, right_ops, preferred_element_type=jn...]
    add x3 -> x0, other arithmetic: 9.77 us -> none  [the longest x1 6.8 us: local(): combined = normal_part + comp_part]
    broadcast_in_dim x2 -> x0, local copies, waits for them, and re-layouts: 4.97 us -> none  [local(): empty = jnp.zeros((sec_dev * width, columns), jnp.float32)]
  transfers between devices with their start and end apart: 2 -> 0, of which waited for: 2 -> 0; matrix products, arithmetic and copies ran while one was open for 0% -> 0% of each run, Pallas kernels for 0% -> 0%
where the time goes in v1:
time: 48.5 us; the launch traced here: 47.8 us
  Pallas kernels  39.9 us (82%)
  local copies, waits for them, and re-layouts  5.73 us (12%)
  other arithmetic  1.44 us (3%)
  between operations  0.68 us (1%)
    pallas_call x1, Pallas kernels, local(): pl.pallas_call(functools.partial(kernel, nz, nx, ns), out_shape=jax.Shape...  39.9 us
    unnamed x8, local copies, waits for them, and re-layouts  4.49 us
    dynamic_slice x1, local copies, waits for them, and re-layouts, local(): kept = sector_rows[first // width]  1.24 us

profile of v1, /device:TPU:4, one launch (start us, length us, event | category | flops | bytes accessed | tf_op | source)
XLA Modules:
  0.0 47.8 jit_solution(11830841523452176230)
XLA Ops:
  0.7 1.2 %dynamic_slice.3 = s32[1]{0:T(128)} dynamic-slice(s32[2]{0:T(128)} %rows_ref.1, s32[]{:T(128)S(6)} %select_n.13), dynamic_slice_sizes={1} | dynamic-slice | bytes 12 | tf_op jit(solution)/shard_map/dynamic_slice | solution.py:323
  1.9 0.7 %add_compare_fusion = pred[128]{0:T(512)(128)(4,1)S(1)} fusion(s32[]{:T(128)} %bitcast, s32[]{:T(128)S(6)} %rem.20), kind=kLoop, calls=%fused_computation.1 | loop fusion | flops 256 | bytes 136 | tf_op jit(solution)/shard_map/lt | solution.py:325
  2.6 0.0 copy-start
  2.6 1.6 %copy-done = bf16[1024,1024]{1,0:T(8,128)(2,1)S(1)} copy-done((bf16[1024,1024]{1,0:T(8,128)(2,1)S(1)}, bf16[1024,1024]{1,0:T(8,128)(2,1)}, u32[]{:S(2)}) %copy-start) | copy-done | bytes 2097176
  4.1 0.0 copy-start.1
  4.1 1.6 %copy-done.1 = bf16[2,2,512,512]{3,2,1,0:T(8,128)(2,1)S(1)} copy-done((bf16[2,2,512,512]{3,2,1,0:T(8,128)(2,1)S(1)}, bf16[2,2,512,512]{3,2,1,0:T(8,128)(2,1)}, u32[]{:S(2)}) %copy-start.1) | copy-done | bytes 2097176
  5.7 0.0 copy-start.2
  5.7 0.7 %copy-done.2 = s32[2]{0:T(128)S(1)} copy-done((s32[2]{0:T(128)S(1)}, s32[2]{0:T(128)}, u32[]{:S(2)}) %copy-start.2) | copy-done | bytes 32
  6.4 0.0 copy-start.3
  6.4 0.7 %copy-done.3 = s32[2]{0:T(128)S(1)} copy-done((s32[2]{0:T(128)S(1)}, s32[2]{0:T(128)}, u32[]{:S(2)}) %copy-start.3) | copy-done | bytes 32
  7.0 39.9 %shard_map.82 = bf16[128,1024]{1,0:T(8,128)(2,1)S(1)} custom-call(s32[2]{0:T(128)S(1)} %copy-done.2, s32[1]{0:T(128)S(6)} %copy.9.count_ref, s32[2]{0:T(128)S(1)} %copy-done.3, bf16[1024,1024]{1,0:T(8,128)(2,1)S(1)} %copy-done, bf16[2,2,512,512]{3,2,1,0:T(8,128)(2,1)S(1)} %copy-done.1, bf16[2,2,512,512]{3,2,1,0:T(8,128)(2,1)} %left_comp.1, ...), custom_call_target="tpu_custom_call" | custom-call | tf_op jit(solution)/shard_map/pallas_call | solution.py:292
  47.0 0.8 %broadcast_select_fusion = bf16[128,1024]{1,0:T(8,128)(2,1)} fusion(bf16[128,1024]{1,0:T(8,128)(2,1)S(1)} %shard_map.82, pred[128]{0:T(512)(128)(4,1)S(1)} %add_compare_fusion), kind=kLoop, calls=%fused_computation | loop fusion | flops 131072 | bytes 524416 | tf_op jit(solution)/shard_map/jit(_where)/select_n | solution.py:325
Async XLA Ops:
  2.6 1.6 %copy-start = (bf16[1024,1024]{1,0:T(8,128)(2,1)S(1)}, bf16[1024,1024]{1,0:T(8,128)(2,1)}, u32[]{:S(2)}) copy-start(bf16[1024,1024]{1,0:T(8,128)(2,1)} %wave.1) | copy-start | bytes 6291460
  4.1 1.6 %copy-start.1 = (bf16[2,2,512,512]{3,2,1,0:T(8,128)(2,1)S(1)}, bf16[2,2,512,512]{3,2,1,0:T(8,128)(2,1)}, u32[]{:S(2)}) copy-start(bf16[2,2,512,512]{3,2,1,0:T(8,128)(2,1)} %left_normal.1) | copy-start | bytes 6291460
  5.7 0.7 %copy-start.2 = (s32[2]{0:T(128)S(1)}, s32[2]{0:T(128)}, u32[]{:S(2)}) copy-start(s32[2]{0:T(128)} %shift_ref.1) | copy-start | bytes 28
  6.4 0.7 %copy-start.3 = (s32[2]{0:T(128)S(1)}, s32[2]{0:T(128)}, u32[]{:S(2)}) copy-start(s32[2]{0:T(128)} %rows_ref.1) | copy-start | bytes 28

commit v2 on v1

--- a/solution.py
+++ b/solution.py
@@ -60,6 +60,9 @@
     x = lax.rem(me, nx)
     partner = z + 1 - 2 * lax.rem(z, 2)
 
+    late = (sect > 0) & (lax.rem(sect, 2) == 0)
+    mirrored = (z >= nz // 2) & jnp.logical_not(late)
+
     loads = {}
 
     def load(name, source, target):
@@ -69,11 +72,12 @@
 
     for s in reversed(range(sec_dev)):
         load(("wave", s), wave.at[pl.ds(s * width, width)], waves.at[s + 1])
-    for s in reversed(range(sec_dev)):
+    for i in range(sec_dev):
+        s = jnp.where(mirrored, i, sec_dev - 1 - i)
         for p in range(pair_dev):
-            load(("normal", s, p), left_normal.at[p, s], lefts.at[0, p, s])
-            load(("comp", s, p), left_comp.at[p, s], lefts.at[1, p, s])
-        if s == sec_dev - 1:
+            load(("normal", i, p), left_normal.at[p, s], lefts.at[0, p, s])
+            load(("comp", i, p), left_comp.at[p, s], lefts.at[1, p, s])
+        if i == 0:
             load("right_comp", right_comp, rights.at[0])
             load("right_normal", right_normal, rights.at[1])
 
@@ -122,7 +126,9 @@
 
     def order(k):
         down = nz - 1 - k
-        return jnp.where(k == nz - 1, z, jnp.where(down > z, down, down - 1))
+        at = jnp.where(mirrored, nz - 1 - z, z)
+        c = jnp.where(k == nz - 1, at, jnp.where(down > at, down, down - 1))
+        return jnp.where(mirrored, nz - 1 - c, c)
 
     def x_copy(c, d, j):
         return pltpu.make_async_remote_copy(
@@ -176,6 +182,12 @@
                     for o in range(1, blocks):
                         piece = jnp.where(offset == o, pieces[(j + o) % blocks], piece)
                     applied[j, kind, p] = piece
+
+        @pl.when(k == 0)
+        def _():
+            loads["right_comp"].wait()
+            loads["right_normal"].wait()
+
         for j in range(blocks):
             result = None
             for kind in range(2):
@@ -213,20 +225,21 @@
                 z_out[c, j] = (own[c, j] + z_in[c, j].astype(F32)).astype(BF16)
                 far_copy(c, j, z // 2).start()
 
-    last = sec_dev - 1
-    for p in range(pair_dev):
-        loads[("normal", last, p)].wait()
-        loads[("comp", last, p)].wait()
-    loads["right_comp"].wait()
-    loads["right_normal"].wait()
-    for s in range(last):
+    def wait_left(i):
         for p in range(pair_dev):
-            loads[("normal", s, p)].wait()
-            loads[("comp", s, p)].wait()
-
-    halo_step = nz - nz // sec_dev - jnp.where(z >= nz // sec_dev, 1, 0)
+            loads[("normal", i, p)].wait()
+            loads[("comp", i, p)].wait()
+
+    wait_left(0)
+    own_late = jnp.where(z >= nz // sec_dev, 1, 0)
+    halo_step = jnp.where(mirrored, 0, nz - nz // sec_dev - own_late)
 
     def step(k, _):
+        @pl.when(k == nz // sec_dev - 1)
+        def _():
+            for i in range(1, sec_dev):
+                wait_left(i)
+
         @pl.when((k == halo_step) & (sect > 0))
         def _():
             halo.wait_recv()
@@ -247,6 +260,9 @@
 
     lax.fori_loop(0, nz + 1, step, 0)
 
+    first = me * part
+    row = lax.broadcasted_iota(jnp.int32, (part, cols), 0) + lax.rem(first, width)
+    kept = row < rows_ref[first // width]
     for j in range(blocks):
         value = own[z, j]
         z_copy(z, j).wait_recv()
@@ -255,7 +271,7 @@
             slot = lax.rem(z // 2 + d, nz // 2)
             far_copy(z, j, slot).wait_recv()
             value = value + far_in[slot, j].astype(F32)
-        out_ref[:, j * cols : (j + 1) * cols] = value.astype(BF16)
+        out_ref[:, j * cols : (j + 1) * cols] = jnp.where(kept, value, 0.0).astype(BF16)
 
     @pl.when(sect < ns - 1)
     def _():
@@ -289,7 +305,7 @@
         dma = pltpu.SemaphoreType.DMA
         smem = pl.BlockSpec(memory_space=pltpu.SMEM)
         hbm = pl.BlockSpec(memory_space=pl.ANY)
-        summed = pl.pallas_call(
+        return pl.pallas_call(
             functools.partial(kernel, nz, nx, ns),
             out_shape=jax.ShapeDtypeStruct((part, blocks * cols), BF16),
             in_specs=[smem] * 3 + [hbm] * 5,
@@ -316,13 +332,9 @@
                 dma((nz // 2, blocks)),
             ],
             compiler_params=pltpu.CompilerParams(
-                collective_id=0, has_side_effects=True, vmem_limit_bytes=48 * 2**20
+                collective_id=0, has_side_effects=True, vmem_limit_bytes=62 * 2**20
             ),
         )(pair_shift, pair_count, sector_rows, wavefunction, left_normal, left_comp, right_comp, right_normal)
-        first = lax.axis_index("pairs") * part
-        kept = sector_rows[first // width]
-        row = lax.broadcasted_iota(jnp.int32, (part, blocks * cols), 0) + lax.rem(first, width)
-        return jnp.where(row < kept, summed, jnp.zeros((), BF16))
 
     placed = (
         P("sect", None),

time: 48.5 us -> 43.8 us (0.903); the launches traced: 47.8 us -> 43.6 us
  local copies, waits for them, and re-layouts: 5.73 us -> 1.67 us
  other arithmetic: 1.44 us -> 0 us
  Pallas kernels: 39.9 us -> 41.3 us
    unnamed x8 -> x1, local copies, waits for them, and re-layouts: 4.49 us -> 1.67 us
    pallas_call x1, Pallas kernels: 39.9 us -> 41.3 us  [local(): pl.pallas_call(functools.partial(kernel, nz, nx, ns), out_shape=jax.Shape...]
    dynamic_slice x1 -> x0, local copies, waits for them, and re-layouts: 1.24 us -> none  [local(): kept = sector_rows[first // width]]
    select_n x1 -> x0, other arithmetic: 0.79 us -> none  [local(): return jnp.where(row < kept, summed, jnp.zeros((), BF16))]
    lt x1 -> x0, other arithmetic: 0.65 us -> none  [local(): return jnp.where(row < kept, summed, jnp.zeros((), BF16))]
where the time goes in v2:
time: 43.8 us; the launch traced here: 43.6 us
  Pallas kernels  41.3 us (94%)
  local copies, waits for them, and re-layouts  1.67 us (4%)
  between operations  0.66 us (2%)
    pallas_call x1, Pallas kernels, local(): pl.pallas_call(functools.partial(kernel, nz, nx, ns), out_shape=jax.Shape...  41.3 us
    unnamed x1, local copies, waits for them, and re-layouts  1.67 us

profile of v2, /device:TPU:4, one launch (start us, length us, event | category | flops | bytes accessed | tf_op | source)
XLA Modules:
  0.0 43.6 jit_solution(18019720256919453836)
XLA Ops:
  0.7 41.3 %shard_map.82 = bf16[128,1024]{1,0:T(8,128)(2,1)} custom-call(s32[2]{0:T(128)} %shift_ref.1, s32[1]{0:T(128)S(6)} %copy.10.count_ref, s32[2]{0:T(128)} %rows_ref.1, bf16[1024,1024]{1,0:T(8,128)(2,1)} %wave.1, bf16[2,2,512,512]{3,2,1,0:T(8,128)(2,1)} %left_normal.1, bf16[2,2,512,512]{3,2,1,0:T(8,128)(2,1)} %left_comp.1, bf16[2,2,512,512]{3,2,1,0:T(8,128)(2,1)} %right_comp.1, ...), custom_call_target="tpu_custom_call" | custom-call | tf_op jit(solution)/shard_map/pallas_call | solution.py:308
  41.9 1.7 %copy.11 = bf16[128,1024]{1,0:T(8,128)(2,1)} copy(bf16[128,1024]{1,0:T(8,128)(2,1)} %shard_map.82) | data formatting | bytes 524288

commit v3 on v2

--- a/solution.py
+++ b/solution.py
@@ -33,7 +33,6 @@
     waves,
     lefts,
     rights,
-    applied,
     total,
     own,
     x_out,
@@ -124,11 +123,16 @@
     for s in reversed(range(sec_dev - 1)):
         mask(s)
 
-    def order(k):
-        down = nz - 1 - k
-        at = jnp.where(mirrored, nz - 1 - z, z)
-        c = jnp.where(k == nz - 1, at, jnp.where(down > at, down, down - 1))
-        return jnp.where(mirrored, nz - 1 - c, c)
+    per_sector = nz // sec_dev
+
+    def sector(i):
+        return jnp.where(mirrored, i, sec_dev - 1 - i)
+
+    def chunk_of(s, q):
+        mine = z - s * per_sector
+        inside = (mine >= 0) & (mine < per_sector)
+        skip = jnp.where(q == per_sector - 1, mine, jnp.where(q < mine, q, q + 1))
+        return s * per_sector + jnp.where(inside, skip, q)
 
     def x_copy(c, d, j):
         return pltpu.make_async_remote_copy(
@@ -165,45 +169,36 @@
         below = (c // 2 < z // 2) & (lax.rem(z, 2) == 0)
         return above | below
 
-    def compute(k):
-        c = order(k)
-        s = c * chunk // width
-        at = pl.ds(pl.multiple_of(c * chunk - s * width, chunk), chunk)
+    def add_terms(s, j, kind):
+        result = None
         for p in range(pair_dev):
-            live = p < count_ref[0]
-            offset = shift_ref[p]
-            for kind in range(2):
-                ops = lefts[kind, p, s, at, :]
-                value = jnp.dot(ops, waves[s + 1 - kind], preferred_element_type=F32)
-                value = jnp.where(live, value, 0.0).astype(BF16)
-                pieces = [value[:, j * cols : (j + 1) * cols] for j in range(blocks)]
-                for j in range(blocks):
-                    piece = pieces[j]
-                    for o in range(1, blocks):
-                        piece = jnp.where(offset == o, pieces[(j + o) % blocks], piece)
-                    applied[j, kind, p] = piece
-
-        @pl.when(k == 0)
-        def _():
-            loads["right_comp"].wait()
-            loads["right_normal"].wait()
-
-        for j in range(blocks):
-            result = None
-            for kind in range(2):
-                for p in range(pair_dev):
-                    term = lax.dot_general(applied[j, kind, p], rights[kind, p, j], NT, preferred_element_type=F32)
-                    result = term if result is None else result + term
-            total[...] = result
-            own[c, j] = total[pl.ds(pl.multiple_of(x * part, part), part), :]
+            block = lax.rem(j + shift_ref[p], blocks)
+            picked = waves[s + 1 - kind, :, :cols]
+            for o in range(1, blocks):
+                picked = jnp.where(block == o, waves[s + 1 - kind, :, o * cols : (o + 1) * cols], picked)
+            value = jnp.dot(lefts[kind, p, s], picked, preferred_element_type=F32)
+            value = jnp.where(p < count_ref[0], value, 0.0).astype(BF16)
+            term = lax.dot_general(value, rights[kind, p, j], NT, preferred_element_type=F32)
+            result = term if result is None else result + term
+        total[j] = result if kind == 0 else total[j] + result
+
+    def send_x(s, j):
+        def send(q, _):
+            c = chunk_of(s, q)
+            start = (c - s * per_sector) * chunk
+            own[c, j] = total[j, pl.ds(pl.multiple_of(start + x * part, part), part), :]
             for d in range(1, nx):
                 to = lax.rem(x + d, nx)
-                x_out[c, d - 1, j] = total[pl.ds(pl.multiple_of(to * part, part), part), :].astype(BF16)
+                rows = pl.ds(pl.multiple_of(start + to * part, part), part)
+                x_out[c, d - 1, j] = total[j, rows, :].astype(BF16)
                 x_copy(c, d, j).start()
-
-    def x_sum(k):
-        c = order(k)
-        for j in range(blocks):
+            return 0
+
+        lax.fori_loop(0, per_sector, send, 0)
+
+    def x_sum(s, j):
+        def add(q, _):
+            c = chunk_of(s, q)
             value = own[c, j]
             for d in range(1, nx):
                 x_copy(c, d, j).wait_recv()
@@ -215,50 +210,69 @@
                 z_out[c, j] = value.astype(BF16)
                 z_copy(c, j).start()
 
-    def z_sum(k):
-        c = order(k)
-
-        @pl.when((c != z) & combines(c))
-        def _():
-            for j in range(blocks):
+            return 0
+
+        lax.fori_loop(0, per_sector, add, 0)
+
+    def z_sum(s, j):
+        def add(q, _):
+            c = chunk_of(s, q)
+
+            @pl.when((c != z) & combines(c))
+            def _():
                 z_copy(c, j).wait_recv()
                 z_out[c, j] = (own[c, j] + z_in[c, j].astype(F32)).astype(BF16)
                 far_copy(c, j, z // 2).start()
 
-    def wait_left(i):
-        for p in range(pair_dev):
-            loads[("normal", i, p)].wait()
-            loads[("comp", i, p)].wait()
-
-    wait_left(0)
-    own_late = jnp.where(z >= nz // sec_dev, 1, 0)
-    halo_step = jnp.where(mirrored, 0, nz - nz // sec_dev - own_late)
-
-    def step(k, _):
-        @pl.when(k == nz // sec_dev - 1)
+            return 0
+
+        lax.fori_loop(0, per_sector, add, 0)
+
+    units = sec_dev * blocks
+
+    def step(t, _):
+        i, j = t // blocks, lax.rem(t, blocks)
+        s = sector(i)
+        for n in range(sec_dev):
+
+            @pl.when(t == n * blocks)
+            def _():
+                for p in range(pair_dev):
+                    loads[("normal", n, p)].wait()
+                    loads[("comp", n, p)].wait()
+                if n == 0:
+                    loads["right_comp"].wait()
+                    loads["right_normal"].wait()
+
+        @pl.when(t < units)
         def _():
-            for i in range(1, sec_dev):
-                wait_left(i)
-
-        @pl.when((k == halo_step) & (sect > 0))
+            begin = jnp.where(i == 0, j, jnp.where(j == 0, 0, blocks))
+            end = jnp.where(i == 0, j + 1, blocks)
+
+            def normal(b, _):
+                add_terms(s, b, 0)
+                return 0
+
+            lax.fori_loop(begin, end, normal, 0)
+
+            @pl.when((s == 0) & (j == 0) & (sect > 0))
+            def _():
+                halo.wait_recv()
+
+            add_terms(s, j, 1)
+            send_x(s, j)
+
+        @pl.when((t >= 1) & (t <= units))
         def _():
-            halo.wait_recv()
-
-        @pl.when(k < nz)
+            x_sum(sector((t - 1) // blocks), lax.rem(t - 1, blocks))
+
+        @pl.when(t >= 2)
         def _():
-            compute(k)
-
-        @pl.when((k >= 1) & (k <= nz))
-        def _():
-            x_sum(k - 1)
-
-        @pl.when(k >= 2)
-        def _():
-            z_sum(k - 2)
+            z_sum(sector((t - 2) // blocks), lax.rem(t - 2, blocks))
 
         return 0
 
-    lax.fori_loop(0, nz + 1, step, 0)
+    lax.fori_loop(0, units + 2, step, 0)
 
     first = me * part
     row = lax.broadcasted_iota(jnp.int32, (part, cols), 0) + lax.rem(first, width)
@@ -271,14 +285,13 @@
             slot = lax.rem(z // 2 + d, nz // 2)
             far_copy(z, j, slot).wait_recv()
             value = value + far_in[slot, j].astype(F32)
-        out_ref[:, j * cols : (j + 1) * cols] = jnp.where(kept, value, 0.0).astype(BF16)
+        out_ref[:, j * cols : (j + 1) * cols] = jnp.where(kept, value, 0.0)
 
     @pl.when(sect < ns - 1)
     def _():
         halo.wait_send()
 
-    def drain(k, _):
-        c = order(k)
+    def drain(c, _):
         for j in range(blocks):
             for d in range(1, nx):
                 x_copy(c, d, j).wait_send()
@@ -307,15 +320,14 @@
         hbm = pl.BlockSpec(memory_space=pl.ANY)
         return pl.pallas_call(
             functools.partial(kernel, nz, nx, ns),
-            out_shape=jax.ShapeDtypeStruct((part, blocks * cols), BF16),
+            out_shape=jax.ShapeDtypeStruct((part, blocks * cols), F32),
             in_specs=[smem] * 3 + [hbm] * 5,
             out_specs=pl.BlockSpec(memory_space=pltpu.VMEM),
             scratch_shapes=[
                 pltpu.VMEM((sec_dev + 1, width, blocks * cols), BF16),
                 pltpu.VMEM((2, pair_dev, sec_dev, width, width), BF16),
                 pltpu.VMEM((2, pair_dev, blocks, cols, cols), BF16),
-                pltpu.VMEM((blocks, 2, pair_dev, chunk, cols), BF16),
-                pltpu.VMEM((chunk, cols), F32),
+                pltpu.VMEM((blocks, width, cols), F32),
                 pltpu.VMEM((nz, blocks, part, cols), F32),
                 pltpu.VMEM((nz, nx - 1, blocks, part, cols), BF16),
                 pltpu.VMEM((nz, nx - 1, blocks, part, cols), BF16),
@@ -334,7 +346,7 @@
             compiler_params=pltpu.CompilerParams(
                 collective_id=0, has_side_effects=True, vmem_limit_bytes=62 * 2**20
             ),
-        )(pair_shift, pair_count, sector_rows, wavefunction, left_normal, left_comp, right_comp, right_normal)
+        )(pair_shift, pair_count, sector_rows, wavefunction, left_normal, left_comp, right_comp, right_normal).astype(BF16)
 
     placed = (
         P("sect", None),

time: 43.8 us -> 44.4 us (1.014); the launches traced: 43.6 us -> 43.6 us
  other arithmetic: 0 us -> 1.78 us
  local copies, waits for them, and re-layouts: 1.67 us -> 0 us
    convert_element_type x0 -> x1, other arithmetic: none -> 1.78 us  [local(): return pl.pallas_call(functools.partial(kernel, nz, nx, ns), out_shape=ja...]
    unnamed x1 -> x0, local copies, waits for them, and re-layouts: 1.67 us -> none
where the time goes in v3:
time: 44.4 us; the launch traced here: 43.6 us
  Pallas kernels  41.2 us (93%)
  other arithmetic  1.78 us (4%)
  between operations  0.66 us (1%)
    pallas_call x1, Pallas kernels, local(): pl.pallas_call(functools.partial(kernel, nz, nx, ns), out_shape=jax.Shape...  41.2 us
    convert_element_type x1, other arithmetic, local(): return pl.pallas_call(functools.partial(kernel, nz, nx, ns), out_shape=ja...  1.78 us

profile of v3, /device:TPU:4, one launch (start us, length us, event | category | flops | bytes accessed | tf_op | source)
XLA Modules:
  0.0 43.6 jit_solution(10941238707798036820)
XLA Ops:
  0.7 41.2 %shard_map.82 = f32[128,1024]{1,0:T(8,128)} custom-call(s32[2]{0:T(128)} %shift_ref.1, s32[1]{0:T(128)S(6)} %copy.9.count_ref, s32[2]{0:T(128)} %rows_ref.1, bf16[1024,1024]{1,0:T(8,128)(2,1)} %wave.1, bf16[2,2,512,512]{3,2,1,0:T(8,128)(2,1)} %left_normal.1, bf16[2,2,512,512]{3,2,1,0:T(8,128)(2,1)} %left_comp.1, bf16[2,2,512,512]{3,2,1,0:T(8,128)(2,1)} %right_comp.1, ...), custom_call_target="tpu_custom_call" | custom-call | tf_op jit(solution)/shard_map/pallas_call | solution.py:321
  41.9 1.8 %convert_element_type.3 = bf16[128,1024]{1,0:T(8,128)(2,1)} convert(f32[128,1024]{1,0:T(8,128)} %shard_map.82) | non-fusion elementwise | flops 131072 | bytes 786432 | tf_op jit(solution)/shard_map/convert_element_type | solution.py:349

commit v4 on v3

--- a/solution.py
+++ b/solution.py
@@ -11,6 +11,7 @@
 F32 = jnp.float32
 BF16 = jnp.bfloat16
 NT = (((1,), (1,)), ((), ()))
+RELAYED = 4
 
 
 def x_size(count):
@@ -60,7 +61,8 @@
     partner = z + 1 - 2 * lax.rem(z, 2)
 
     late = (sect > 0) & (lax.rem(sect, 2) == 0)
-    mirrored = (z >= nz // 2) & jnp.logical_not(late)
+    mirrored = z >= nz // 2
+    half = lax.rem(z, 2) * RELAYED
 
     loads = {}
 
@@ -103,18 +105,28 @@
 
     mask(sec_dev - 1)
     pl.semaphore_wait(barrier, nx - 1 + nz - 1 + 2)
-    halo = pltpu.make_async_remote_copy(
-        src_ref=waves.at[sec_dev],
-        dst_ref=waves.at[0],
-        send_sem=halo_send,
-        recv_sem=halo_recv,
-        device_id=(me, lax.rem(sect + 1, ns)),
-        device_id_type=MESH,
-    )
+    piece = width // (2 * RELAYED)
+
+    def halo_copy(r, relay):
+        rows = pl.ds(pl.multiple_of(r * piece, piece), piece)
+        return pltpu.make_async_remote_copy(
+            src_ref=waves.at[0 if relay else sec_dev, rows],
+            dst_ref=waves.at[0, rows],
+            send_sem=halo_send.at[r + 2 * RELAYED if relay else r],
+            recv_sem=halo_recv.at[r],
+            device_id=(partner * nx + x, sect) if relay else (me, lax.rem(sect + 1, ns)),
+            device_id_type=MESH,
+        )
+
+    crosses = lax.rem(sect, 2) == 1
 
     @pl.when(sect < ns - 1)
     def _():
-        halo.start()
+        def send(r, _):
+            halo_copy(r, False).start()
+            return 0
+
+        lax.fori_loop(jnp.where(crosses, half, 0), jnp.where(crosses, half + RELAYED, 2 * RELAYED), send, 0)
 
     @pl.when(sect == 0)
     def _():
@@ -246,18 +258,34 @@
 
         @pl.when(t < units)
         def _():
-            begin = jnp.where(i == 0, j, jnp.where(j == 0, 0, blocks))
-            end = jnp.where(i == 0, j + 1, blocks)
+            single = (i == 0) & jnp.logical_not(late)
+            begin = jnp.where(single, j, jnp.where(j == 0, 0, blocks))
+            end = jnp.where(single, j + 1, blocks)
 
             def normal(b, _):
                 add_terms(s, b, 0)
+
+                @pl.when((t == 0) & late)
+                def _():
+                    each = RELAYED // blocks
+                    for r in range(each):
+                        at = half + b * each + r
+                        halo_copy(at, False).wait_recv()
+                        halo_copy(at, True).start()
+
                 return 0
 
             lax.fori_loop(begin, end, normal, 0)
 
             @pl.when((s == 0) & (j == 0) & (sect > 0))
             def _():
-                halo.wait_recv()
+                other = RELAYED - half
+
+                def wait(r, _):
+                    halo_copy(r, False).wait_recv()
+                    return 0
+
+                lax.fori_loop(jnp.where(late, other, 0), jnp.where(late, other + RELAYED, 2 * RELAYED), wait, 0)
 
             add_terms(s, j, 1)
             send_x(s, j)
@@ -289,7 +317,19 @@
 
     @pl.when(sect < ns - 1)
     def _():
-        halo.wait_send()
+        def sent(r, _):
+            halo_copy(r, False).wait_send()
+            return 0
+
+        lax.fori_loop(jnp.where(crosses, half, 0), jnp.where(crosses, half + RELAYED, 2 * RELAYED), sent, 0)
+
+    @pl.when(late)
+    def _():
+        def sent(r, _):
+            halo_copy(r, True).wait_send()
+            return 0
+
+        lax.fori_loop(half, half + RELAYED, sent, 0)
 
     def drain(c, _):
         for j in range(blocks):
@@ -335,8 +375,8 @@
                 pltpu.VMEM((nz, blocks, part, cols), BF16),
                 pltpu.VMEM((nz // 2, blocks, part, cols), BF16),
                 dma((sec_dev + 2 * sec_dev * pair_dev + 2,)),
-                dma,
-                dma,
+                dma((4 * RELAYED,)),
+                dma((2 * RELAYED,)),
                 dma((nz, nx - 1, blocks)),
                 dma((nz, nx - 1, blocks)),
                 dma((nz, blocks)),
@@ -344,7 +384,7 @@
                 dma((nz // 2, blocks)),
             ],
             compiler_params=pltpu.CompilerParams(
-                collective_id=0, has_side_effects=True, vmem_limit_bytes=62 * 2**20
+                collective_id=0, has_side_effects=True, vmem_limit_bytes=61 * 2**20
             ),
         )(pair_shift, pair_count, sector_rows, wavefunction, left_normal, left_comp, right_comp, right_normal).astype(BF16)
 

time: 44.4 us -> 45.1 us (1.016)
  the two profiles are of different devices: /device:TPU:4 before, /device:TPU:14 now
where the time goes in v4:
time: 45.1 us; the launch traced here: 44.9 us
  Pallas kernels  42.5 us (94%)
  other arithmetic  1.78 us (4%)
  between operations  0.66 us (1%)
    pallas_call x1, Pallas kernels, local(): pl.pallas_call(functools.partial(kernel, nz, nx, ns), out_shape=jax.Shape...  42.5 us
    convert_element_type x1, other arithmetic, local(): return pl.pallas_call(functools.partial(kernel, nz, nx, ns), out_shape=ja...  1.78 us

profile of v4, /device:TPU:14, one launch (start us, length us, event | category | flops | bytes accessed | tf_op | source)
XLA Modules:
  0.0 44.9 jit_solution(5922356240158619196)
XLA Ops:
  0.7 42.5 %shard_map.82 = f32[128,1024]{1,0:T(8,128)} custom-call(s32[2]{0:T(128)} %shift_ref.1, s32[1]{0:T(128)S(6)} %copy.9.count_ref, s32[2]{0:T(128)} %rows_ref.1, bf16[1024,1024]{1,0:T(8,128)(2,1)} %wave.1, bf16[2,2,512,512]{3,2,1,0:T(8,128)(2,1)} %left_normal.1, bf16[2,2,512,512]{3,2,1,0:T(8,128)(2,1)} %left_comp.1, bf16[2,2,512,512]{3,2,1,0:T(8,128)(2,1)} %right_comp.1, ...), custom_call_target="tpu_custom_call" | custom-call | tf_op jit(solution)/shard_map/pallas_call | solution.py:361
  43.2 1.8 %convert_element_type.3 = bf16[128,1024]{1,0:T(8,128)(2,1)} convert(f32[128,1024]{1,0:T(8,128)} %shard_map.82) | non-fusion elementwise | flops 131072 | bytes 786432 | tf_op jit(solution)/shard_map/convert_element_type | solution.py:389

commit v5 on v3

--- a/solution.py
+++ b/solution.py
@@ -31,6 +31,7 @@
     right_normal,
     out_ref,
     waves,
+    relay,
     lefts,
     rights,
     total,
@@ -85,7 +86,7 @@
         pl.semaphore_signal(barrier, inc=1, device_id=(z * nx + lax.rem(x + d, nx), sect), device_id_type=MESH)
     for d in range(1, nz):
         pl.semaphore_signal(barrier, inc=1, device_id=(lax.rem(z + d, nz) * nx + x, sect), device_id_type=MESH)
-    for d in (1, ns - 1):
+    for d in (1, ns - 1, 2, ns - 2):
         pl.semaphore_signal(barrier, inc=1, device_id=(me, lax.rem(sect + d, ns)), device_id_type=MESH)
 
     def mask(s):
@@ -102,19 +103,39 @@
         lax.fori_loop(0, width // step, body, 0)
 
     mask(sec_dev - 1)
-    pl.semaphore_wait(barrier, nx - 1 + nz - 1 + 2)
-    halo = pltpu.make_async_remote_copy(
-        src_ref=waves.at[sec_dev],
-        dst_ref=waves.at[0],
-        send_sem=halo_send,
-        recv_sem=halo_recv,
-        device_id=(me, lax.rem(sect + 1, ns)),
-        device_id_type=MESH,
-    )
-
-    @pl.when(sect < ns - 1)
-    def _():
-        halo.start()
+    pl.semaphore_wait(barrier, nx - 1 + nz - 1 + 4)
+    top, bottom = pl.ds(0, width // 2), pl.ds(width // 2, width // 2)
+
+    def halo_copy(n, source, rows, target, to):
+        return pltpu.make_async_remote_copy(
+            src_ref=source.at[rows],
+            dst_ref=target.at[rows],
+            send_sem=halo_send.at[n],
+            recv_sem=halo_recv.at[n],
+            device_id=(me, lax.rem(to, ns)),
+            device_id_type=MESH,
+        )
+
+    odd = lax.rem(sect, 2) == 1
+    sends, crosses = sect < ns - 1, (sect < ns - 1) & odd
+    relays = (sect < ns - 2) & jnp.logical_not(odd)
+    held = relay.at[0]
+    top_copy = halo_copy(0, waves.at[sec_dev], top, waves.at[0], sect + 1)
+    bottom_copy = halo_copy(1, waves.at[sec_dev], bottom, waves.at[0], sect + 1)
+    back_copy = halo_copy(2, waves.at[sec_dev], bottom, held, sect + ns - 1)
+    relay_copy = halo_copy(3, held, bottom, waves.at[0], sect + 2)
+
+    @pl.when(crosses)
+    def _():
+        back_copy.start()
+
+    @pl.when(sends)
+    def _():
+        top_copy.start()
+
+    @pl.when(sends & jnp.logical_not(odd))
+    def _():
+        bottom_copy.start()
 
     @pl.when(sect == 0)
     def _():
@@ -251,13 +272,27 @@
 
             def normal(b, _):
                 add_terms(s, b, 0)
+
+                @pl.when((t == 0) & relays)
+                def _():
+                    back_copy.wait_recv()
+                    relay_copy.start()
+
                 return 0
 
             lax.fori_loop(begin, end, normal, 0)
 
             @pl.when((s == 0) & (j == 0) & (sect > 0))
             def _():
-                halo.wait_recv()
+                top_copy.wait_recv()
+
+                @pl.when(odd)
+                def _():
+                    bottom_copy.wait_recv()
+
+                @pl.when(late)
+                def _():
+                    relay_copy.wait_recv()
 
             add_terms(s, j, 1)
             send_x(s, j)
@@ -287,9 +322,21 @@
             value = value + far_in[slot, j].astype(F32)
         out_ref[:, j * cols : (j + 1) * cols] = jnp.where(kept, value, 0.0)
 
-    @pl.when(sect < ns - 1)
-    def _():
-        halo.wait_send()
+    @pl.when(crosses)
+    def _():
+        back_copy.wait_send()
+
+    @pl.when(sends)
+    def _():
+        top_copy.wait_send()
+
+    @pl.when(sends & jnp.logical_not(odd))
+    def _():
+        bottom_copy.wait_send()
+
+    @pl.when(relays)
+    def _():
+        relay_copy.wait_send()
 
     def drain(c, _):
         for j in range(blocks):
@@ -317,7 +364,7 @@
         part = chunk // nx
         dma = pltpu.SemaphoreType.DMA
         smem = pl.BlockSpec(memory_space=pltpu.SMEM)
-        hbm = pl.BlockSpec(memory_space=pl.ANY)
+        hbm = pl.BlockSpec(memory_space=pltpu.HBM)
         return pl.pallas_call(
             functools.partial(kernel, nz, nx, ns),
             out_shape=jax.ShapeDtypeStruct((part, blocks * cols), F32),
@@ -325,6 +372,7 @@
             out_specs=pl.BlockSpec(memory_space=pltpu.VMEM),
             scratch_shapes=[
                 pltpu.VMEM((sec_dev + 1, width, blocks * cols), BF16),
+                pltpu.VMEM((1, width, blocks * cols), BF16),
                 pltpu.VMEM((2, pair_dev, sec_dev, width, width), BF16),
                 pltpu.VMEM((2, pair_dev, blocks, cols, cols), BF16),
                 pltpu.VMEM((blocks, width, cols), F32),
@@ -335,8 +383,8 @@
                 pltpu.VMEM((nz, blocks, part, cols), BF16),
                 pltpu.VMEM((nz // 2, blocks, part, cols), BF16),
                 dma((sec_dev + 2 * sec_dev * pair_dev + 2,)),
-                dma,
-                dma,
+                dma((4,)),
+                dma((4,)),
                 dma((nz, nx - 1, blocks)),
                 dma((nz, nx - 1, blocks)),
                 dma((nz, blocks)),
@@ -344,7 +392,7 @@
                 dma((nz // 2, blocks)),
             ],
             compiler_params=pltpu.CompilerParams(
-                collective_id=0, has_side_effects=True, vmem_limit_bytes=62 * 2**20
+                collective_id=0, has_side_effects=True, vmem_limit_bytes=60 * 2**20
             ),
         )(pair_shift, pair_count, sector_rows, wavefunction, left_normal, left_comp, right_comp, right_normal).astype(BF16)
 

time: 44.4 us -> 44.5 us (level)
  no operation moved by 1% of the time
where the time goes in v5:
time: 44.5 us; the launch traced here: 43.7 us
  Pallas kernels  41.3 us (93%)
  other arithmetic  1.78 us (4%)
  between operations  0.66 us (1%)
    pallas_call x1, Pallas kernels, local(): pl.pallas_call(functools.partial(kernel, nz, nx, ns), out_shape=jax.Shape...  41.3 us
    convert_element_type x1, other arithmetic, local(): return pl.pallas_call(functools.partial(kernel, nz, nx, ns), out_shape=ja...  1.78 us

profile of v5, /device:TPU:4, one launch (start us, length us, event | category | flops | bytes accessed | tf_op | source)
XLA Modules:
  0.0 43.7 jit_solution(12350140147584091584)
XLA Ops:
  0.7 41.3 %shard_map.82 = f32[128,1024]{1,0:T(8,128)} custom-call(s32[2]{0:T(128)} %shift_ref.1, s32[1]{0:T(128)S(6)} %copy.9.count_ref, s32[2]{0:T(128)} %rows_ref.1, bf16[1024,1024]{1,0:T(8,128)(2,1)} %wave.1, bf16[2,2,512,512]{3,2,1,0:T(8,128)(2,1)} %left_normal.1, bf16[2,2,512,512]{3,2,1,0:T(8,128)(2,1)} %left_comp.1, bf16[2,2,512,512]{3,2,1,0:T(8,128)(2,1)} %right_comp.1, ...), custom_call_target="tpu_custom_call" | custom-call | tf_op jit(solution)/shard_map/pallas_call | solution.py:368
  41.9 1.8 %convert_element_type.3 = bf16[128,1024]{1,0:T(8,128)(2,1)} convert(f32[128,1024]{1,0:T(8,128)} %shard_map.82) | non-fusion elementwise | flops 131072 | bytes 786432 | tf_op jit(solution)/shard_map/convert_element_type | solution.py:397

commit v6 on v3

--- a/solution.py
+++ b/solution.py
@@ -75,9 +75,11 @@
         s = jnp.where(mirrored, i, sec_dev - 1 - i)
         for p in range(pair_dev):
             load(("normal", i, p), left_normal.at[p, s], lefts.at[0, p, s])
+        if i == 0:
+            load("right_comp", right_comp, rights.at[0])
+        for p in range(pair_dev):
             load(("comp", i, p), left_comp.at[p, s], lefts.at[1, p, s])
         if i == 0:
-            load("right_comp", right_comp, rights.at[0])
             load("right_normal", right_normal, rights.at[1])
 
     barrier = pltpu.get_barrier_semaphore()
@@ -94,9 +96,11 @@
 
         def body(i, _):
             at = pl.ds(i * step, step)
-            keep = lax.broadcasted_iota(jnp.int32, (step, blocks * cols), 0) + i * step < rows_ref[s]
-            value = waves[s + 1, at, :].astype(F32)
-            waves[s + 1, at, :] = jnp.where(keep, value, 0.0).astype(BF16)
+            row = lax.broadcasted_iota(jnp.int32, (step, 128), 0) + i * step
+            keep = jnp.where(row < rows_ref[s], 1.0, 0.0).astype(BF16)
+            for first in range(0, blocks * cols, 128):
+                columns = slice(first, first + 128)
+                waves[s + 1, at, columns] = waves[s + 1, at, columns] * keep
             return 0
 
         lax.fori_loop(0, width // step, body, 0)
@@ -229,23 +233,31 @@
         lax.fori_loop(0, per_sector, add, 0)
 
     units = sec_dev * blocks
+    moved = late & (z >= nz // 2)
+
+    def unit(t):
+        there = jnp.where(t == 0, 0, jnp.where(t == units - 1, 1, t + 1))
+        index = jnp.where(moved, there, t)
+        return index // blocks, lax.rem(index, blocks)
+
+    def wait_loads(i, j, name, right):
+        for n in range(sec_dev):
+
+            @pl.when((i == n) & (j == 0))
+            def _():
+                for p in range(pair_dev):
+                    loads[(name, n, p)].wait()
+                if n == 0:
+                    loads[right].wait()
 
     def step(t, _):
-        i, j = t // blocks, lax.rem(t, blocks)
+        i, j = unit(t)
         s = sector(i)
-        for n in range(sec_dev):
-
-            @pl.when(t == n * blocks)
-            def _():
-                for p in range(pair_dev):
-                    loads[("normal", n, p)].wait()
-                    loads[("comp", n, p)].wait()
-                if n == 0:
-                    loads["right_comp"].wait()
-                    loads["right_normal"].wait()
 
         @pl.when(t < units)
         def _():
+            wait_loads(i, j, "normal", "right_comp")
+
             begin = jnp.where(i == 0, j, jnp.where(j == 0, 0, blocks))
             end = jnp.where(i == 0, j + 1, blocks)
 
@@ -254,6 +266,7 @@
                 return 0
 
             lax.fori_loop(begin, end, normal, 0)
+            wait_loads(i, j, "comp", "right_normal")
 
             @pl.when((s == 0) & (j == 0) & (sect > 0))
             def _():
@@ -264,11 +277,13 @@
 
         @pl.when((t >= 1) & (t <= units))
         def _():
-            x_sum(sector((t - 1) // blocks), lax.rem(t - 1, blocks))
+            i, j = unit(t - 1)
+            x_sum(sector(i), j)
 
         @pl.when(t >= 2)
         def _():
-            z_sum(sector((t - 2) // blocks), lax.rem(t - 2, blocks))
+            i, j = unit(t - 2)
+            z_sum(sector(i), j)
 
         return 0
 

time: 44.4 us -> 43.4 us (0.977)
  Pallas kernels: 41.2 us -> 40.3 us
    pallas_call x1, Pallas kernels: 41.2 us -> 40.3 us  [local(): pl.pallas_call(functools.partial(kernel, nz, nx, ns), out_shape=jax.Shape...]
where the time goes in v6:
time: 43.4 us; the launch traced here: 42.7 us
  Pallas kernels  40.3 us (93%)
  other arithmetic  1.78 us (4%)
  between operations  0.66 us (2%)
    pallas_call x1, Pallas kernels, local(): pl.pallas_call(functools.partial(kernel, nz, nx, ns), out_shape=jax.Shape...  40.3 us
    convert_element_type x1, other arithmetic, local(): return pl.pallas_call(functools.partial(kernel, nz, nx, ns), out_shape=ja...  1.78 us

profile of v6, /device:TPU:4, one launch (start us, length us, event | category | flops | bytes accessed | tf_op | source)
XLA Modules:
  0.0 42.7 jit_solution(1717312773422388534)
XLA Ops:
  0.7 40.3 %shard_map.82 = f32[128,1024]{1,0:T(8,128)} custom-call(s32[2]{0:T(128)} %shift_ref.1, s32[1]{0:T(128)S(6)} %copy.9.count_ref, s32[2]{0:T(128)} %rows_ref.1, bf16[1024,1024]{1,0:T(8,128)(2,1)} %wave.1, bf16[2,2,512,512]{3,2,1,0:T(8,128)(2,1)} %left_normal.1, bf16[2,2,512,512]{3,2,1,0:T(8,128)(2,1)} %left_comp.1, bf16[2,2,512,512]{3,2,1,0:T(8,128)(2,1)} %right_comp.1, ...), custom_call_target="tpu_custom_call" | custom-call | tf_op jit(solution)/shard_map/pallas_call | solution.py:336
  40.9 1.8 %convert_element_type.3 = bf16[128,1024]{1,0:T(8,128)(2,1)} convert(f32[128,1024]{1,0:T(8,128)} %shard_map.82) | non-fusion elementwise | flops 131072 | bytes 786432 | tf_op jit(solution)/shard_map/convert_element_type | solution.py:364

commit v7 on v6

--- a/solution.py
+++ b/solution.py
@@ -173,32 +173,28 @@
         below = (c // 2 < z // 2) & (lax.rem(z, 2) == 0)
         return above | below
 
-    def add_terms(s, j, kind):
+    def add_terms(s, j, kind, rows=slice(None)):
         result = None
         for p in range(pair_dev):
             block = lax.rem(j + shift_ref[p], blocks)
             picked = waves[s + 1 - kind, :, :cols]
             for o in range(1, blocks):
                 picked = jnp.where(block == o, waves[s + 1 - kind, :, o * cols : (o + 1) * cols], picked)
-            value = jnp.dot(lefts[kind, p, s], picked, preferred_element_type=F32)
+            value = jnp.dot(lefts[kind, p, s, rows], picked, preferred_element_type=F32)
             value = jnp.where(p < count_ref[0], value, 0.0).astype(BF16)
             term = lax.dot_general(value, rights[kind, p, j], NT, preferred_element_type=F32)
             result = term if result is None else result + term
-        total[j] = result if kind == 0 else total[j] + result
-
-    def send_x(s, j):
-        def send(q, _):
-            c = chunk_of(s, q)
-            start = (c - s * per_sector) * chunk
-            own[c, j] = total[j, pl.ds(pl.multiple_of(start + x * part, part), part), :]
-            for d in range(1, nx):
-                to = lax.rem(x + d, nx)
-                rows = pl.ds(pl.multiple_of(start + to * part, part), part)
-                x_out[c, d - 1, j] = total[j, rows, :].astype(BF16)
-                x_copy(c, d, j).start()
-            return 0
-
-        lax.fori_loop(0, per_sector, send, 0)
+        total[j, rows] = result if kind == 0 else total[j, rows] + result
+
+    def send_x(s, j, q):
+        c = chunk_of(s, q)
+        start = (c - s * per_sector) * chunk
+        own[c, j] = total[j, pl.ds(pl.multiple_of(start + x * part, part), part), :]
+        for d in range(1, nx):
+            to = lax.rem(x + d, nx)
+            rows = pl.ds(pl.multiple_of(start + to * part, part), part)
+            x_out[c, d - 1, j] = total[j, rows, :].astype(BF16)
+            x_copy(c, d, j).start()
 
     def x_sum(s, j):
         def add(q, _):
@@ -254,7 +250,25 @@
         i, j = unit(t)
         s = sector(i)
 
-        @pl.when(t < units)
+        def wait_halo():
+            @pl.when((s == 0) & (j == 0) & (sect > 0))
+            def _():
+                halo.wait_recv()
+
+        @pl.when(t == 0)
+        def _():
+            wait_loads(i, j, "normal", "right_comp")
+            for q in range(per_sector):
+                start = (chunk_of(s, q) - s * per_sector) * chunk
+                rows = pl.ds(pl.multiple_of(start, chunk), chunk)
+                add_terms(s, j, 0, rows)
+                if q == 0:
+                    wait_loads(i, j, "comp", "right_normal")
+                    wait_halo()
+                add_terms(s, j, 1, rows)
+                send_x(s, j, q)
+
+        @pl.when((t > 0) & (t < units))
         def _():
             wait_loads(i, j, "normal", "right_comp")
 
@@ -267,23 +281,24 @@
 
             lax.fori_loop(begin, end, normal, 0)
             wait_loads(i, j, "comp", "right_normal")
-
-            @pl.when((s == 0) & (j == 0) & (sect > 0))
-            def _():
-                halo.wait_recv()
-
+            wait_halo()
             add_terms(s, j, 1)
-            send_x(s, j)
+
+            def send(q, _):
+                send_x(s, j, q)
+                return 0
+
+            lax.fori_loop(0, per_sector, send, 0)
+
+        @pl.when(t >= 2)
+        def _():
+            i, j = unit(t - 2)
+            z_sum(sector(i), j)
 
         @pl.when((t >= 1) & (t <= units))
         def _():
             i, j = unit(t - 1)
             x_sum(sector(i), j)
-
-        @pl.when(t >= 2)
-        def _():
-            i, j = unit(t - 2)
-            z_sum(sector(i), j)
 
         return 0
 

time: 43.4 us -> 43.3 us (level)
  the two profiles are of different devices: /device:TPU:4 before, /device:TPU:12 now
where the time goes in v7:
time: 43.3 us; the launch traced here: 43.1 us
  Pallas kernels  40.7 us (94%)
  other arithmetic  1.78 us (4%)
  between operations  0.66 us (2%)
    pallas_call x1, Pallas kernels, local(): pl.pallas_call(functools.partial(kernel, nz, nx, ns), out_shape=jax.Shape...  40.7 us
    convert_element_type x1, other arithmetic, local(): return pl.pallas_call(functools.partial(kernel, nz, nx, ns), out_shape=ja...  1.78 us

profile of v7, /device:TPU:12, one launch (start us, length us, event | category | flops | bytes accessed | tf_op | source)
XLA Modules:
  0.0 43.1 jit_solution(14953393800611013039)
XLA Ops:
  0.7 40.7 %shard_map.82 = f32[128,1024]{1,0:T(8,128)} custom-call(s32[2]{0:T(128)} %shift_ref.1, s32[1]{0:T(128)S(6)} %copy.9.count_ref, s32[2]{0:T(128)} %rows_ref.1, bf16[1024,1024]{1,0:T(8,128)(2,1)} %wave.1, bf16[2,2,512,512]{3,2,1,0:T(8,128)(2,1)} %left_normal.1, bf16[2,2,512,512]{3,2,1,0:T(8,128)(2,1)} %left_comp.1, bf16[2,2,512,512]{3,2,1,0:T(8,128)(2,1)} %right_comp.1, ...), custom_call_target="tpu_custom_call" | custom-call | tf_op jit(solution)/shard_map/pallas_call | solution.py:351
  41.3 1.8 %convert_element_type.3 = bf16[128,1024]{1,0:T(8,128)(2,1)} convert(f32[128,1024]{1,0:T(8,128)} %shard_map.82) | non-fusion elementwise | flops 131072 | bytes 786432 | tf_op jit(solution)/shard_map/convert_element_type | solution.py:379

commit v8 on v2

--- a/solution.py
+++ b/solution.py
@@ -76,6 +76,7 @@
         s = jnp.where(mirrored, i, sec_dev - 1 - i)
         for p in range(pair_dev):
             load(("normal", i, p), left_normal.at[p, s], lefts.at[0, p, s])
+        for p in range(pair_dev):
             load(("comp", i, p), left_comp.at[p, s], lefts.at[1, p, s])
         if i == 0:
             load("right_comp", right_comp, rights.at[0])
@@ -95,9 +96,11 @@
 
         def body(i, _):
             at = pl.ds(i * step, step)
-            keep = lax.broadcasted_iota(jnp.int32, (step, blocks * cols), 0) + i * step < rows_ref[s]
-            value = waves[s + 1, at, :].astype(F32)
-            waves[s + 1, at, :] = jnp.where(keep, value, 0.0).astype(BF16)
+            row = lax.broadcasted_iota(jnp.int32, (step, 128), 0) + i * step
+            keep = jnp.where(row < rows_ref[s], 1.0, 0.0).astype(BF16)
+            for first in range(0, blocks * cols, 128):
+                columns = slice(first, first + 128)
+                waves[s + 1, at, columns] = waves[s + 1, at, columns] * keep
             return 0
 
         lax.fori_loop(0, width // step, body, 0)
@@ -165,14 +168,37 @@
         below = (c // 2 < z // 2) & (lax.rem(z, 2) == 0)
         return above | below
 
+    def wait_left(i, kind):
+        for p in range(pair_dev):
+            loads[(("normal", "comp")[kind], i, p)].wait()
+
+    own_late = jnp.where(z >= nz // sec_dev, 1, 0)
+    halo_step = jnp.where(mirrored, 0, nz - nz // sec_dev - own_late)
+
     def compute(k):
         c = order(k)
         s = c * chunk // width
         at = pl.ds(pl.multiple_of(c * chunk - s * width, chunk), chunk)
-        for p in range(pair_dev):
-            live = p < count_ref[0]
-            offset = shift_ref[p]
-            for kind in range(2):
+        for kind in range(2):
+
+            @pl.when(k == 0)
+            def _():
+                wait_left(0, kind)
+
+            @pl.when(k == nz // sec_dev - 1)
+            def _():
+                for i in range(1, sec_dev):
+                    wait_left(i, kind)
+
+            if kind == 1:
+
+                @pl.when((k == halo_step) & (sect > 0))
+                def _():
+                    halo.wait_recv()
+
+            for p in range(pair_dev):
+                live = p < count_ref[0]
+                offset = shift_ref[p]
                 ops = lefts[kind, p, s, at, :]
                 value = jnp.dot(ops, waves[s + 1 - kind], preferred_element_type=F32)
                 value = jnp.where(live, value, 0.0).astype(BF16)
@@ -225,36 +251,18 @@
                 z_out[c, j] = (own[c, j] + z_in[c, j].astype(F32)).astype(BF16)
                 far_copy(c, j, z // 2).start()
 
-    def wait_left(i):
-        for p in range(pair_dev):
-            loads[("normal", i, p)].wait()
-            loads[("comp", i, p)].wait()
-
-    wait_left(0)
-    own_late = jnp.where(z >= nz // sec_dev, 1, 0)
-    halo_step = jnp.where(mirrored, 0, nz - nz // sec_dev - own_late)
-
     def step(k, _):
-        @pl.when(k == nz // sec_dev - 1)
-        def _():
-            for i in range(1, sec_dev):
-                wait_left(i)
-
-        @pl.when((k == halo_step) & (sect > 0))
-        def _():
-            halo.wait_recv()
-
         @pl.when(k < nz)
         def _():
             compute(k)
 
+        @pl.when(k >= 2)
+        def _():
+            z_sum(k - 2)
+
         @pl.when((k >= 1) & (k <= nz))
         def _():
             x_sum(k - 1)
-
-        @pl.when(k >= 2)
-        def _():
-            z_sum(k - 2)
 
         return 0
 

time: 43.8 us -> 43.6 us (level)
  no operation moved by 1% of the time
where the time goes in v8:
time: 43.6 us; the launch traced here: 43.4 us
  Pallas kernels  41.1 us (94%)
  local copies, waits for them, and re-layouts  1.67 us (4%)
  between operations  0.66 us (2%)
    pallas_call x1, Pallas kernels, local(): pl.pallas_call(functools.partial(kernel, nz, nx, ns), out_shape=jax.Shape...  41.1 us
    unnamed x1, local copies, waits for them, and re-layouts  1.67 us

profile of v8, /device:TPU:4, one launch (start us, length us, event | category | flops | bytes accessed | tf_op | source)
XLA Modules:
  0.0 43.4 jit_solution(4501377650736927108)
XLA Ops:
  0.7 41.1 %shard_map.82 = bf16[128,1024]{1,0:T(8,128)(2,1)} custom-call(s32[2]{0:T(128)} %shift_ref.1, s32[1]{0:T(128)S(6)} %copy.10.count_ref, s32[2]{0:T(128)} %rows_ref.1, bf16[1024,1024]{1,0:T(8,128)(2,1)} %wave.1, bf16[2,2,512,512]{3,2,1,0:T(8,128)(2,1)} %left_normal.1, bf16[2,2,512,512]{3,2,1,0:T(8,128)(2,1)} %left_comp.1, bf16[2,2,512,512]{3,2,1,0:T(8,128)(2,1)} %right_comp.1, ...), custom_call_target="tpu_custom_call" | custom-call | tf_op jit(solution)/shard_map/pallas_call | solution.py:316
  41.7 1.7 %copy.11 = bf16[128,1024]{1,0:T(8,128)(2,1)} copy(bf16[128,1024]{1,0:T(8,128)(2,1)} %shard_map.82) | data formatting | bytes 524288

commit v9 on v8

--- a/solution.py
+++ b/solution.py
@@ -62,6 +62,7 @@
 
     late = (sect > 0) & (lax.rem(sect, 2) == 0)
     mirrored = (z >= nz // 2) & jnp.logical_not(late)
+    straight = (z >= nz // 2) & late
 
     loads = {}
 
@@ -166,7 +167,7 @@
     def combines(c):
         above = (c // 2 > z // 2) & (lax.rem(z, 2) == 1)
         below = (c // 2 < z // 2) & (lax.rem(z, 2) == 0)
-        return above | below
+        return (above | below) & jnp.logical_not(straight)
 
     def wait_left(i, kind):
         for p in range(pair_dev):
@@ -239,7 +240,15 @@
             @pl.when((c != z) & jnp.logical_not(combines(c)))
             def _():
                 z_out[c, j] = value.astype(BF16)
-                z_copy(c, j).start()
+                far = straight & (c // 2 != z // 2)
+
+                @pl.when(far)
+                def _():
+                    far_copy(c, j, z).start()
+
+                @pl.when(jnp.logical_not(far))
+                def _():
+                    z_copy(c, j).start()
 
     def z_sum(k):
         c = order(k)
@@ -249,7 +258,7 @@
             for j in range(blocks):
                 z_copy(c, j).wait_recv()
                 z_out[c, j] = (own[c, j] + z_in[c, j].astype(F32)).astype(BF16)
-                far_copy(c, j, z // 2).start()
+                far_copy(c, j, z).start()
 
     def step(k, _):
         @pl.when(k < nz)
@@ -276,9 +285,21 @@
         z_copy(z, j).wait_recv()
         value = value + z_in[z, j].astype(F32)
         for d in range(1, nz // 2):
-            slot = lax.rem(z // 2 + d, nz // 2)
-            far_copy(z, j, slot).wait_recv()
-            value = value + far_in[slot, j].astype(F32)
+            pair = lax.rem(z // 2 + d, nz // 2)
+            inner = 2 * pair + jnp.where(pair < z // 2, 1, 0)
+            far_copy(z, j, inner).wait_recv()
+            value = value + far_in[inner, j].astype(F32)
+        own[z, j] = value
+        for d in range(1, nz // 2):
+            pair = lax.rem(z // 2 + d, nz // 2)
+            outer = 2 * pair + jnp.where(pair < z // 2, 0, 1)
+
+            @pl.when(late & (2 * pair >= nz // 2))
+            def _():
+                far_copy(z, j, outer).wait_recv()
+                own[z, j] = own[z, j] + far_in[outer, j].astype(F32)
+
+        value = own[z, j]
         out_ref[:, j * cols : (j + 1) * cols] = jnp.where(kept, value, 0.0).astype(BF16)
 
     @pl.when(sect < ns - 1)
@@ -329,7 +350,7 @@
                 pltpu.VMEM((nz, nx - 1, blocks, part, cols), BF16),
                 pltpu.VMEM((nz, blocks, part, cols), BF16),
                 pltpu.VMEM((nz, blocks, part, cols), BF16),
-                pltpu.VMEM((nz // 2, blocks, part, cols), BF16),
+                pltpu.VMEM((nz, blocks, part, cols), BF16),
                 dma((sec_dev + 2 * sec_dev * pair_dev + 2,)),
                 dma,
                 dma,
@@ -337,7 +358,7 @@
                 dma((nz, nx - 1, blocks)),
                 dma((nz, blocks)),
                 dma((nz, blocks)),
-                dma((nz // 2, blocks)),
+                dma((nz, blocks)),
             ],
             compiler_params=pltpu.CompilerParams(
                 collective_id=0, has_side_effects=True, vmem_limit_bytes=62 * 2**20

time: 43.6 us -> 42.6 us (0.977)
  Pallas kernels: 41.1 us -> 40.1 us
    pallas_call x1, Pallas kernels: 41.1 us -> 40.1 us  [local(): pl.pallas_call(functools.partial(kernel, nz, nx, ns), out_shape=jax.Shape...]
where the time goes in v9:
time: 42.6 us; the launch traced here: 42.4 us
  Pallas kernels  40.1 us (94%)
  local copies, waits for them, and re-layouts  1.67 us (4%)
  between operations  0.66 us (2%)
    pallas_call x1, Pallas kernels, local(): pl.pallas_call(functools.partial(kernel, nz, nx, ns), out_shape=jax.Shape...  40.1 us
    unnamed x1, local copies, waits for them, and re-layouts  1.67 us

profile of v9, /device:TPU:4, one launch (start us, length us, event | category | flops | bytes accessed | tf_op | source)
XLA Modules:
  0.0 42.4 jit_solution(15906231644424822365)
XLA Ops:
  0.7 40.1 %shard_map.82 = bf16[128,1024]{1,0:T(8,128)(2,1)} custom-call(s32[2]{0:T(128)} %shift_ref.1, s32[1]{0:T(128)S(6)} %copy.10.count_ref, s32[2]{0:T(128)} %rows_ref.1, bf16[1024,1024]{1,0:T(8,128)(2,1)} %wave.1, bf16[2,2,512,512]{3,2,1,0:T(8,128)(2,1)} %left_normal.1, bf16[2,2,512,512]{3,2,1,0:T(8,128)(2,1)} %left_comp.1, bf16[2,2,512,512]{3,2,1,0:T(8,128)(2,1)} %right_comp.1, ...), custom_call_target="tpu_custom_call" | custom-call | tf_op jit(solution)/shard_map/pallas_call | solution.py:337
  40.7 1.7 %copy.11 = bf16[128,1024]{1,0:T(8,128)(2,1)} copy(bf16[128,1024]{1,0:T(8,128)(2,1)} %shard_map.82) | data formatting | bytes 524288

commit v10 on v9

--- a/solution.py
+++ b/solution.py
@@ -261,6 +261,12 @@
                 far_copy(c, j, z).start()
 
     def step(k, _):
+        early = straight & (k == nz - 1)
+
+        @pl.when(early)
+        def _():
+            x_sum(k - 1)
+
         @pl.when(k < nz)
         def _():
             compute(k)
@@ -269,7 +275,7 @@
         def _():
             z_sum(k - 2)
 
-        @pl.when((k >= 1) & (k <= nz))
+        @pl.when((k >= 1) & (k <= nz) & jnp.logical_not(early))
         def _():
             x_sum(k - 1)
 

time: 42.6 us -> 42.6 us (level)
  no operation moved by 1% of the time
where the time goes in v10:
time: 42.6 us; the launch traced here: 42.4 us
  Pallas kernels  40.1 us (94%)
  local copies, waits for them, and re-layouts  1.67 us (4%)
  between operations  0.66 us (2%)
    pallas_call x1, Pallas kernels, local(): pl.pallas_call(functools.partial(kernel, nz, nx, ns), out_shape=jax.Shape...  40.1 us
    unnamed x1, local copies, waits for them, and re-layouts  1.67 us

profile of v10, /device:TPU:4, one launch (start us, length us, event | category | flops | bytes accessed | tf_op | source)
XLA Modules:
  0.0 42.4 jit_solution(13633687878991902158)
XLA Ops:
  0.7 40.1 %shard_map.82 = bf16[128,1024]{1,0:T(8,128)(2,1)} custom-call(s32[2]{0:T(128)} %shift_ref.1, s32[1]{0:T(128)S(6)} %copy.10.count_ref, s32[2]{0:T(128)} %rows_ref.1, bf16[1024,1024]{1,0:T(8,128)(2,1)} %wave.1, bf16[2,2,512,512]{3,2,1,0:T(8,128)(2,1)} %left_normal.1, bf16[2,2,512,512]{3,2,1,0:T(8,128)(2,1)} %left_comp.1, bf16[2,2,512,512]{3,2,1,0:T(8,128)(2,1)} %right_comp.1, ...), custom_call_target="tpu_custom_call" | custom-call | tf_op jit(solution)/shard_map/pallas_call | solution.py:343
  40.8 1.7 %copy.11 = bf16[128,1024]{1,0:T(8,128)(2,1)} copy(bf16[128,1024]{1,0:T(8,128)(2,1)} %shard_map.82) | data formatting | bytes 524288
